TPU v7x, 32 devices: a whole 2x2x4 slice. The times are simulated.
32 devices in a mesh: ta: 4 (over z), ha: 2 (over y), wa: 4 (over x, core).
Axes of the slice: x: 2, y: 2, z: 4, core: 2. Of those that a mesh axis runs over, the one named last changes fastest.
Arguments:
- stream: bfloat16 [4, 2, 384, 1536], P('ta', 'ha'), may hold values from -40 to 40
- queries: bfloat16 [4, 2, 384, 1536], P('ta', 'ha', None, 'wa'), may hold values from -6 to 6
- key_heads: bfloat16 [4, 2, 384, 1536], P('ta', 'ha', None, 'wa'), may hold values from -6 to 6
- value_heads: bfloat16 [4, 2, 384, 1536], P('ta', 'ha', None, 'wa'), may hold values from -6 to 6
- out_weight: bfloat16 [1536, 1536], P('wa'), may hold values from -0.15625 to 0.15625
- norm_gain: float32 [1536], replicated, may hold values from 0.25 to 1.75
- up_weight: bfloat16 [1536, 6144], P(('ta', 'ha'), 'wa'), may hold values from -0.15625 to 0.15625
- down_weight: bfloat16 [6144, 1536], P('wa', ('ta', 'ha')), may hold values from -0.078125 to 0.078125
- tile_route: int32 [4, 2, 1], P('ta', 'ha'), may hold values 0 or 1
- cotangent: bfloat16 [4, 2, 384, 1536], P('ta', 'ha'), may hold values from -6 to 6
Outputs:
- stream_grad: bfloat16 [4, 2, 384, 1536], P('ta', 'ha')
- query_grad: bfloat16 [4, 2, 384, 1536], P('ta', 'ha', None, 'wa')
- key_grad: bfloat16 [4, 2, 384, 1536], P('ta', 'ha', None, 'wa')
- value_grad: bfloat16 [4, 2, 384, 1536], P('ta', 'ha', None, 'wa')
- out_weight_grad: float32 [1536, 1536], P('wa', ('ta', 'ha'))
All inputs are finite; a program needn't handle non-finite values. No bound on the sum of `tile_route` on one device may be relied on, other than what follows from the above.
Results may differ from a plain program's by a relative error of at most 0.014.
Values may be sent and summed in bfloat16 or wider, within the bound.
A program may use at most 128 MiB of HBM per device.

v0:
```python
import math
import jax
import jax.numpy as jnp
from jax import lax
from jax.sharding import PartitionSpec as P

HS = 128
TILE = 384
EPSILON = 1e-06
TANH_SCALE = 0.7978845608028654
CUBIC_COEF = 0.044715
NEG_FILL = -1e30


def extended(cells, sides, width):
    for axis, dim in sides:
        count = lax.axis_size(axis)
        ends = count - 1
        head = lax.slice_in_dim(cells, 0, width, axis=dim)
        tail = lax.slice_in_dim(cells, cells.shape[dim] - width, cells.shape[dim], axis=dim)
        cells = jnp.concatenate(
            [
                lax.ppermute(tail, axis, [(i, (i + 1) % count) for i in range(ends)]),
                cells,
                lax.ppermute(head, axis, [((i + 1) % count, i) for i in range(ends)]),
            ],
            axis=dim,
        )
    return cells


def from_behind(array, axis, by):
    devices = lax.axis_size(axis)
    pairs = [(i, i + by) for i in range(devices) if 0 <= i + by < devices]
    return lax.ppermute(array, axis, pairs)


def gelu_slope(pre_act):
    tanh_arg = TANH_SCALE * (pre_act + CUBIC_COEF * pre_act * pre_act * pre_act)
    tanh_val = jnp.tanh(tanh_arg)
    return 0.5 * (1.0 + tanh_val) + 0.5 * pre_act * (1.0 - tanh_val * tanh_val) * TANH_SCALE * (
        1.0 + 3.0 * CUBIC_COEF * pre_act * pre_act
    )


def head_probs(query_rows, key_rows, key_marks, score_scale):
    scores = (
        jnp.einsum("qd,kd->qk", query_rows, key_rows, preferred_element_type=jnp.float32)
        * score_scale
    )
    scores = jnp.where(key_marks[None, :] > 0.5, scores, NEG_FILL)
    row_max = jnp.max(scores, axis=1)
    weights = jnp.exp(scores - row_max[:, None])
    row_total = jnp.sum(weights, axis=1)
    return (weights / row_total[:, None], row_max, row_total)


def layer_norm(residual):
    mean_val = jnp.mean(residual, axis=1, keepdims=True)
    centered = residual - mean_val
    variance = jnp.mean(centered * centered, axis=1, keepdims=True)
    inv_std = lax.rsqrt(variance + EPSILON)
    return (centered * inv_std, inv_std)


def norm_backward(norm_grad, norm_gain, normed, inv_std):
    scaled = norm_grad * norm_gain
    return (
        scaled
        - jnp.mean(scaled, axis=1, keepdims=True)
        - normed * jnp.mean(scaled * normed, axis=1, keepdims=True)
    ) * inv_std


def shards(
    stream,
    queries,
    key_heads,
    value_heads,
    out_weight,
    norm_gain,
    up_weight,
    down_weight,
    tile_route,
    cotangent,
):
    row_count = stream.shape[2]
    model_width = stream.shape[3]
    channels = queries.shape[3]
    heads_here = channels // HS
    tile_count = row_count // TILE
    score_scale = 1.0 / math.sqrt(HS)
    tile_ids = jnp.arange(tile_count, dtype=jnp.int32)
    tile_marks = tile_route.astype(jnp.bfloat16)
    faces_key, faces_value, faces_marks = (
        extended(key_heads, (("ta", 0), ("ha", 1)), 1),
        extended(value_heads, (("ta", 0), ("ha", 1)), 1),
        extended(tile_marks, (("ta", 0), ("ha", 1)), 1),
    )

    def window():
        key_block = faces_key.reshape(9 * TILE, heads_here, HS)
        value_block = faces_value.reshape(9 * TILE, heads_here, HS)
        mark_block = faces_marks.reshape(9).astype(jnp.float32)
        key_marks = jnp.repeat(mark_block, TILE)
        query_tile = queries.reshape(TILE, heads_here, HS)
        return (
            query_tile.transpose(1, 0, 2),
            key_block.transpose(1, 0, 2),
            value_block.transpose(1, 0, 2),
            key_marks,
        )

    def forward_tile(tile_index):
        own_mark = tile_marks[0, 0, tile_index]
        query_tile, key_block, value_block, key_marks = window()

        def per_head(operands):
            query_rows, key_rows, value_rows = operands
            weights, row_max, row_total = head_probs(query_rows, key_rows, key_marks, score_scale)
            mixture = jnp.dot(
                weights.astype(jnp.bfloat16), value_rows, preferred_element_type=jnp.float32
            )
            return (mixture, row_max, row_total)

        mixture, row_max, row_total = lax.map(per_head, (query_tile, key_block, value_block))
        scaled = (mixture * own_mark.astype(jnp.float32)).astype(jnp.bfloat16)
        return (scaled.transpose(1, 0, 2).reshape(TILE, channels), row_max, row_total)

    attn_tiles, max_tiles, total_tiles = lax.map(forward_tile, tile_ids)
    attention = attn_tiles.reshape(row_count, channels)
    attn_part = jnp.dot(attention, out_weight, preferred_element_type=jnp.float32)
    head_share = lax.psum_scatter(attn_part, "wa", scatter_dimension=0, tiled=True)
    share_rows = head_share.shape[0]
    share_start = lax.axis_index("wa") * share_rows
    flat_stream = stream.reshape(row_count, model_width)
    flat_cot = cotangent.reshape(row_count, model_width)
    residual = (
        lax.dynamic_slice_in_dim(flat_stream, share_start, share_rows, 0).astype(jnp.float32)
        + head_share
    )
    normed, inv_std = layer_norm(residual)
    hidden_share = (normed * norm_gain).astype(jnp.bfloat16)
    hidden_in = lax.all_gather(hidden_share, "wa", axis=0, tiled=True)
    up_full, down_full = (
        lax.all_gather(up_weight, ("ta", "ha"), axis=0, tiled=True),
        lax.all_gather(down_weight, ("ta", "ha"), axis=1, tiled=True),
    )
    pre_act = jnp.dot(hidden_in, up_full, preferred_element_type=jnp.float32)
    act_grad = jnp.einsum("td,fd->tf", flat_cot, down_full, preferred_element_type=jnp.float32)
    pre_grad = (act_grad * gelu_slope(pre_act)).astype(jnp.bfloat16)
    norm_part = jnp.einsum("tf,df->td", pre_grad, up_full, preferred_element_type=jnp.float32)
    norm_share = lax.psum_scatter(norm_part, "wa", scatter_dimension=0, tiled=True)
    cot_share = lax.dynamic_slice_in_dim(flat_cot, share_start, share_rows, 0).astype(jnp.float32)
    grad_share = (cot_share + norm_backward(norm_share, norm_gain, normed, inv_std)).astype(
        jnp.bfloat16
    )
    stream_grad = lax.all_gather(grad_share, "wa", axis=0, tiled=True)
    weight_part = jnp.einsum(
        "tc,td->cd", attention, stream_grad, preferred_element_type=jnp.float32
    )
    out_weight_grad = lax.psum_scatter(weight_part, ("ta", "ha"), scatter_dimension=1, tiled=True)
    attn_grad = jnp.einsum(
        "td,cd->tc", stream_grad, out_weight, preferred_element_type=jnp.float32
    ).astype(jnp.bfloat16)
    row_marks = jnp.repeat(tile_marks.reshape(tile_count), TILE)
    masked_grad = attn_grad * row_marks[:, None]

    def own_side():
        query_tile, key_block, value_block, key_marks = window()
        grad_tile = masked_grad.reshape(TILE, heads_here, HS).transpose(1, 0, 2)

        def head_back(operands):
            query_rows, key_rows, value_rows, grad_rows = operands
            weights = head_probs(query_rows, key_rows, key_marks, score_scale)[0]
            grad_probs = jnp.einsum(
                "qd,kd->qk", grad_rows, value_rows, preferred_element_type=jnp.float32
            )
            row_delta = jnp.sum(weights * grad_probs, axis=1)
            grad_scores = (weights * (grad_probs - row_delta[:, None]) * score_scale).astype(
                jnp.bfloat16
            )
            query_part = jnp.dot(grad_scores, key_rows, preferred_element_type=jnp.float32).astype(
                jnp.bfloat16
            )
            value_part = jnp.einsum(
                "qk,qd->kd",
                weights.astype(jnp.bfloat16),
                grad_rows,
                preferred_element_type=jnp.float32,
            ).astype(jnp.bfloat16)
            key_part = jnp.einsum(
                "qk,qd->kd", grad_scores, query_rows, preferred_element_type=jnp.float32
            ).astype(jnp.bfloat16)
            return (query_part, row_delta, key_part, value_part)

        results = lax.map(head_back, (query_tile, key_block, value_block, grad_tile))
        query_part = results[0].transpose(1, 0, 2).reshape(TILE, channels)
        key_part = results[2].transpose(1, 0, 2).reshape(3, 3, TILE, channels)
        value_part = results[3].transpose(1, 0, 2).reshape(3, 3, TILE, channels)
        return (query_part, results[1], key_part, value_part)

    def guarded_own():
        blank_parts = (
            jnp.zeros((TILE, channels), jnp.bfloat16),
            jnp.zeros((heads_here, TILE), jnp.float32),
        )
        blank_parts = blank_parts + (
            jnp.zeros((3, 3, TILE, channels), jnp.bfloat16),
            jnp.zeros((3, 3, TILE, channels), jnp.bfloat16),
        )
        return own_side()

    def place_tile(carried, tile_index):
        query_part, row_delta, key_part, value_part = guarded_own()
        return ((key_part, value_part), query_part)

    empty_slots = jnp.zeros((3, 3, row_count, channels), jnp.bfloat16)
    (slots_key, slots_value), query_parts = lax.scan(
        place_tile, (empty_slots, empty_slots), tile_ids
    )
    middle_key = slots_key[1].astype(jnp.float32)
    middle_value = slots_value[1].astype(jnp.float32)
    for by_step, source in ((-1, 0), (1, 2)):
        moved_key, moved_value = from_behind(
            (slots_key[source], slots_value[source]), "ta", by_step
        )
        middle_key = middle_key + moved_key.astype(jnp.float32)
        middle_value = middle_value + moved_value.astype(jnp.float32)
    final_key = middle_key[1]
    final_value = middle_value[1]
    for by_step, source in ((-1, 0), (1, 2)):
        moved_key, moved_value = (
            from_behind(middle_key[source].astype(jnp.bfloat16), "ha", by_step).astype(jnp.float32),
            from_behind(middle_value[source].astype(jnp.bfloat16), "ha", by_step).astype(
                jnp.float32
            ),
        )
        final_key = final_key + moved_key
        final_value = final_value + moved_value
    key_grad = final_key.astype(jnp.bfloat16).reshape(1, 1, row_count, channels)
    value_grad = final_value.astype(jnp.bfloat16).reshape(1, 1, row_count, channels)
    query_grad = query_parts.reshape(1, 1, row_count, channels)
    return (
        stream_grad.reshape(1, 1, row_count, model_width),
        query_grad,
        key_grad,
        value_grad,
        out_weight_grad,
    )


def solution(mesh):
    placed = (
        P("ta", "ha", None, None),
        P("ta", "ha", None, "wa"),
        P("ta", "ha", None, "wa"),
        P("ta", "ha", None, "wa"),
        P("wa", None),
        P(),
        P(("ta", "ha"), "wa"),
        P("wa", ("ta", "ha")),
        P("ta", "ha", None),
        P("ta", "ha", None, None),
    )
    return jax.shard_map(
        shards,
        mesh=mesh,
        in_specs=placed,
        out_specs=(
            P("ta", "ha", None, None),
            P("ta", "ha", None, "wa"),
            P("ta", "ha", None, "wa"),
            P("ta", "ha", None, "wa"),
            P("wa", ("ta", "ha")),
        ),
        check_vma=False,
    )
```

profile of v0, /device:TPU:0, one launch (start us, length us, event | category | flops | bytes accessed | tf_op | source)
XLA Modules:
  0.0 548.8 jit_solution(6073854629250690570)
XLA Ops:
  7.2 5.1 collective-permute-start.8
  13.6 4.6 collective-permute-start.4
  20.9 3.0 collective-permute-done.9
  23.9 4.4 collective-permute-start.10
  30.7 6.4 %collective-permute-start.6 = (bf16[3,1,384,384]{3,2,1,0:T(8,128)(2,1)S(1)}, bf16[3,1,384,384]{3,2,1,0:T(8,128)(2,1)}, u32[]{:S(2)}, u32[]{:S(2)}) collective-permute-start(bf16[3,1,384,384]{3,2,1,0:T(8,128)(2,1)S(1)} %constant_dynamic-update-slice_fusion.1), channel_id=1, source_target_pairs={{0,4},{1,5},{2,6},{3,7},{8,12},{9,13},{10,14},{11,15},{16,20},{17,... | collective-permute-start | bytes 2654216 | tf_op jit(solution)/shard_map/ppermute | solution.py:23
  39.0 4.8 collective-permute-start
  45.6 4.1 collective-permute-done.1
  51.0 5.5 collective-permute-start.2
  56.6 6.5 %collective-permute-done.2 = bf16[3,1,1]{0,2,1:T(2,128)(2,1)S(1)} collective-permute-done((bf16[3,1,1]{0,2,1:T(2,128)(2,1)S(1)}, bf16[3,1,1]{0,2,1:T(2,128)(2,1)S(1)}, u32[]{:S(2)}, u32[]{:S(2)}) %collective-permute-start.2) | collective-permute-done | bytes 38 | tf_op jit(solution)/shard_map/ppermute | solution.py:23
  64.5 4.0 collective-permute-done.3
  68.8 3.3 pad_maximum_fusion.1
  72.1 7.7 %reshape.147 = bf16[3456,3,128]{2,1,0:T(4,128)(2,1)} reshape(bf16[3,3,384,384]{3,2,1,0:T(8,128)(2,1)} %pad_maximum_fusion.1) | data formatting | bytes 5308416 | tf_op jit(solution)/shard_map/while/body/eval_jaxpr/reshape | solution.py:103
  79.8 3.9 copy.47
  83.7 3.3 pad_maximum_fusion
  87.0 7.7 %reshape.146 = bf16[3456,3,128]{2,1,0:T(4,128)(2,1)} reshape(bf16[3,3,384,384]{3,2,1,0:T(8,128)(2,1)} %pad_maximum_fusion) | data formatting | bytes 5308416 | tf_op jit(solution)/shard_map/while/body/eval_jaxpr/reshape | solution.py:102
  94.7 3.9 copy.46
  98.7 16.9 %while.44 = (s32[]{:T(128)}, f32[3,384,128]{1,2,0:T(8,128)S(1)}, bf16[3,384,128]{2,1,0:T(8,128)(2,1)S(1)}, bf16[3,3456,128]{2,1,0:T(8,128)(2,1)}, bf16[3,3456,128]{2,1,0:T(8,128)(2,1)}, /*index=5*/f32[9]{0:T(128)S(1)}, s32[]{:T(128)}) while((s32[]{:T(128)}, f32[3,384,128]{1,2,0:T(8,128)S(1)}, bf16[3,384,128]{2,1,0:T(8,128)(2,1)S(1)}, ...), condition=%wide.region_3.4_spmd.clone, body=%wide.region_0.3_spmd.clone.sunk | while | flops 690093312 | bytes 18014980 | solution.py:126
  98.8 2.2 fusion.110
  101.8 2.5 fusion.112
  104.4 2.2 fusion.110
  107.5 2.5 fusion.112
  110.1 2.2 fusion.110
  113.1 2.5 fusion.112
  115.7 2.2 fusion.79
  118.0 32.4 %reduce-scatter.4.cloned.1.call-done = f32[96,1536]{1,0:T(8,128)} async-done(((f32[384,1536]{1,0:T(8,128)}), f32[96,1536]{1,0:T(8,128)}) %reduce-scatter.4.cloned.1.call-update) | async-done | bytes 589840 | tf_op jit(solution)/shard_map/reduce_scatter | solution.py:133
  154.7 15.8 %all-gather.7.cloned.1.call-done = bf16[384,1536]{1,0:T(8,128)(2,1)} async-done(((bf16[96,1536]{1,0:T(8,128)(2,1)}), bf16[384,1536]{1,0:T(8,128)(2,1)}) %all-gather.7.cloned.1.call-update) | async-done | bytes 1179664 | tf_op jit(solution)/shard_map/all_gather | solution.py:144
  170.5 82.3 %all-gather.9.cloned.1.call-done = bf16[1536,1536]{1,0:T(8,128)(2,1)} async-done(((bf16[192,1536]{1,0:T(8,128)(2,1)}), bf16[1536,1536]{1,0:T(8,128)(2,1)}) %all-gather.9.cloned.1.call-update) | async-done | bytes 4718608 | tf_op jit(solution)/shard_map/all_gather | solution.py:146
  252.8 6.1 %fusion.80 = f32[384,1536]{1,0:T(8,128)} fusion(bf16[384,1536]{1,0:T(8,128)(2,1)} %all-gather.7.cloned.1.call-done, bf16[1536,1536]{1,0:T(8,128)(2,1)} %all-gather.9.cloned.1.call-done), kind=kOutput, calls=%fused_computation.124 | convolution fusion | flops 1811939328 | bytes 8257536 | tf_op jit(solution)/shard_map/dot_general | solution.py:149
  258.9 74.3 %all-gather.5.cloned.1.call-done = bf16[1536,1536]{0,1:T(8,128)(2,1)} async-done(((bf16[1536,192]{0,1:T(8,128)(2,1)}), bf16[1536,1536]{0,1:T(8,128)(2,1)}) %all-gather.5.cloned.1.call-update) | async-done | bytes 4718608 | tf_op jit(solution)/shard_map/all_gather | solution.py:147
  333.1 10.0 %fusion.56 = f32[384,1536]{1,0:T(8,128)} fusion(bf16[1536,1536]{1,0:T(8,128)(2,1)} %all-gather.9.cloned.1.call-done, bf16[1536,1536]{0,1:T(8,128)(2,1)} %all-gather.5.cloned.1.call-done, f32[384,1536]{1,0:T(8,128)} %fusion.80, bf16[1,1,384,1536]{3,2,1,0:T(8,128)(2,1)} %param.23), kind=kOutput, calls=%fused_computation.75 | convolution fusion | flops 3635085312 | bytes 15335424 | tf_op jit(solution)/shard_map/tf,df->td/dot_general | solution.py:152
  343.3 31.3 %reduce-scatter.6.cloned.1.call-done = f32[96,1536]{1,0:T(8,128)} async-done(((f32[384,1536]{1,0:T(8,128)}), f32[96,1536]{1,0:T(8,128)}) %reduce-scatter.6.cloned.1.call-update) | async-done | bytes 589840 | tf_op jit(solution)/shard_map/reduce_scatter | solution.py:153
  375.9 2.2 fusion.64
  378.2 17.5 %all-gather.11.cloned.1.call-done = bf16[384,1536]{1,0:T(8,128)(2,1)} async-done(((bf16[96,1536]{1,0:T(8,128)(2,1)}), bf16[384,1536]{1,0:T(8,128)(2,1)}) %all-gather.11.cloned.1.call-update) | async-done | bytes 1179664 | tf_op jit(solution)/shard_map/all_gather | solution.py:158
  395.8 2.2 fusion.54
  398.2 2.3 fusion.81
  400.5 43.7 %while.45 = (s32[]{:T(128)}, bf16[3,384,128]{1,2,0:T(8,128)(2,1)S(1)}, bf16[3,3456,128]{2,1,0:T(8,128)(2,1)}, bf16[3,3456,128]{2,1,0:T(8,128)(2,1)}, bf16[3,384,...) while((s32[]{:T(128)}, ...), condition=%wide.region_14.15_spmd.clone, body=%wide.region_10.14_spmd.clone.sunk | while | flops 1723513728 | bytes 71701848 | solution.py:197
  400.6 2.2 fusion.119
  403.7 2.2 fusion.123
  405.9 2.5 multiply_reduce_fusion.5
  412.9 2.0 fusion.121
  415.2 2.2 fusion.119
  418.2 2.2 fusion.123
  420.4 2.5 multiply_reduce_fusion.5
  429.8 2.2 fusion.119
  432.8 2.2 fusion.123
  435.1 2.5 multiply_reduce_fusion.5
  442.1 2.0 fusion.121
  444.3 2.9 fusion.77
  447.1 5.5 copy.58
  456.0 5.6 %copy.59 = bf16[1152,3,128]{2,1,0:T(4,128)(2,1)S(1)} copy(bf16[1152,3,128]{2,0,1:T(8,128)(2,1)} %get-tuple-element.257) | data formatting | bytes 1769472 | tf_op jit(solution)/shard_map/slice | solution.py:226
  463.6 5.5 collective-permute-start.17
  469.1 3.4 fusion.78
  472.5 5.5 copy.55
  481.3 5.6 %copy.56 = bf16[1152,3,128]{2,1,0:T(4,128)(2,1)S(1)} copy(bf16[1152,3,128]{2,0,1:T(8,128)(2,1)} %get-tuple-element.260) | data formatting | bytes 1769472 | tf_op jit(solution)/shard_map/slice | solution.py:226
  488.9 5.7 %collective-permute-start.13 = (bf16[3,384,384]{2,1,0:T(8,128)(2,1)}, bf16[3,384,384]{2,1,0:T(8,128)(2,1)}, u32[]{:S(2)}, u32[]{:S(2)}) collective-permute-start(bf16[3,384,384]{2,1,0:T(8,128)(2,1)} %squeeze.56), channel_id=1, source_target_pairs={{0,8},{8,16},{16,24},{1,9},{9,17},{17,25},{2,10},{10,18},{18,26},{... | collective-permute-start | bytes 2654216 | tf_op jit(solution)/shard_map/ppermute | solution.py:35
  494.6 5.9 %copy.57 = f32[1152,3,128]{2,1,0:T(4,128)} copy(f32[1152,3,128]{2,0,1:T(8,128)S(1)} %get-tuple-element.258) | data formatting | bytes 3538944 | tf_op jit(solution)/shard_map/convert_element_type | solution.py:223
  500.5 4.3 reshape.158
  504.8 5.9 %copy.54 = f32[1152,3,128]{2,1,0:T(4,128)} copy(f32[1152,3,128]{2,0,1:T(8,128)S(1)} %copy-done.2) | data formatting | bytes 3538944 | tf_op jit(solution)/shard_map/convert_element_type | solution.py:222
  510.6 3.0 reshape.157
  513.6 3.5 fusion.72
  519.2 5.3 collective-permute-start.19
  524.5 2.9 fusion.73
  529.5 5.3 collective-permute-start.15
  535.7 2.1 fusion.66
  (142 shorter events, 59.7 us)
Async XLA Ops:
  7.2 108.5 %copy-start = (bf16[384,1536]{1,0:T(8,128)(2,1)S(1)}, bf16[384,1536]{1,0:T(8,128)(2,1)}, u32[]{:S(2)}) copy-start(bf16[384,1536]{1,0:T(8,128)(2,1)} %param.18) | copy-start | bytes 3538948
  7.2 36.6 %copy-start.8 = (bf16[1,1,384,384]{3,2,1,0:T(8,128)(2,1)S(1)}, bf16[1,1,384,384]{3,2,1,0:T(8,128)(2,1)}, u32[]{:S(2)}) copy-start(bf16[1,1,384,384]{3,2,1,0:T(8,128)(2,1)} %param.15) | copy-start | bytes 884740
  7.2 143.2 %reduce-scatter.4.cloned.1.call-start = ((), (), s32[]{:S(2)}) async-start(), calls=%async_computation.4 | async-start | bytes 2949120 | tf_op jit(solution)/shard_map/reduce_scatter | solution.py:133
  7.2 12.6 %collective-permute-start.8 = (bf16[1,1,384,384]{3,2,1,0:T(8,128)(2,1)}, bf16[1,1,384,384]{3,2,1,0:T(8,128)(2,1)S(1)}, u32[]{:S(2)}, u32[]{:S(2)}) collective-permute-start(bf16[1,1,384,384]{3,2,1,0:T(8,128)(2,1)} %param.17), channel_id=1, source_target_pairs={{0,8},{8,16},{16,24},{1,9},{9,17},{17,25},{2,10},{10,18},{18,26},{... | collective-permute-start | bytes 884744 | tf_op jit(solution)/shard_map/ppermute | solution.py:23
  12.3 11.5 %collective-permute-start.9 = (bf16[1,1,384,384]{3,2,1,0:T(8,128)(2,1)}, bf16[1,1,384,384]{3,2,1,0:T(8,128)(2,1)S(1)}, u32[]{:S(2)}, u32[]{:S(2)}) collective-permute-start(bf16[1,1,384,384]{3,2,1,0:T(8,128)(2,1)} %param.17), channel_id=1, source_target_pairs={{8,0},{16,8},{24,16},{9,1},{17,9},{25,17},{10,2},{18,10},{26,18},{... | collective-permute-start | bytes 884744 | tf_op jit(solution)/shard_map/ppermute | solution.py:25
  13.6 15.9 %collective-permute-start.4 = (bf16[1,1,384,384]{3,2,1,0:T(8,128)(2,1)}, bf16[1,1,384,384]{3,2,1,0:T(8,128)(2,1)S(1)}, u32[]{:S(2)}, u32[]{:S(2)}) collective-permute-start(bf16[1,1,384,384]{3,2,1,0:T(8,128)(2,1)} %param.16), channel_id=1, source_target_pairs={{0,8},{8,16},{16,24},{1,9},{9,17},{17,25},{2,10},{10,18},{18,26},{... | collective-permute-start | bytes 884744 | tf_op jit(solution)/shard_map/ppermute | solution.py:23
  18.2 12.4 %collective-permute-start.5 = (bf16[1,1,384,384]{3,2,1,0:T(8,128)(2,1)}, bf16[1,1,384,384]{3,2,1,0:T(8,128)(2,1)S(1)}, u32[]{:S(2)}, u32[]{:S(2)}) collective-permute-start(bf16[1,1,384,384]{3,2,1,0:T(8,128)(2,1)} %param.16), channel_id=1, source_target_pairs={{8,0},{16,8},{24,16},{9,1},{17,9},{25,17},{10,2},{18,10},{26,18},{... | collective-permute-start | bytes 884744 | tf_op jit(solution)/shard_map/ppermute | solution.py:25
  23.9 44.9 %collective-permute-start.10 = (bf16[3,1,384,384]{3,2,1,0:T(8,128)(2,1)S(1)}, bf16[3,1,384,384]{3,2,1,0:T(8,128)(2,1)}, u32[]{:S(2)}, u32[]{:S(2)}) collective-permute-start(bf16[3,1,384,384]{3,2,1,0:T(8,128)(2,1)S(1)} %constant_dynamic-update-slice_fusion.4), channel_id=1, source_target_pairs={{0,4},{1,5},{2,6},{3,7},{8,12},{9,13},{10,14},{11,15},{16,20},{17,... | collective-permute-start | bytes 2654216 | tf_op jit(solution)/shard_map/ppermute | solution.py:23
  28.3 40.5 %collective-permute-start.11 = (bf16[3,1,384,384]{3,2,1,0:T(8,128)(2,1)S(1)}, bf16[3,1,384,384]{3,2,1,0:T(8,128)(2,1)}, u32[]{:S(2)}, u32[]{:S(2)}) collective-permute-start(bf16[3,1,384,384]{3,2,1,0:T(8,128)(2,1)S(1)} %constant_dynamic-update-slice_fusion.4), channel_id=1, source_target_pairs={{4,0},{5,1},{6,2},{7,3},{12,8},{13,9},{14,10},{15,11},{20,16},{21,... | collective-permute-start | bytes 2654216 | tf_op jit(solution)/shard_map/ppermute | solution.py:25
  30.7 53.0 %collective-permute-start.6 = (bf16[3,1,384,384]{3,2,1,0:T(8,128)(2,1)S(1)}, bf16[3,1,384,384]{3,2,1,0:T(8,128)(2,1)}, u32[]{:S(2)}, u32[]{:S(2)}) collective-permute-start(bf16[3,1,384,384]{3,2,1,0:T(8,128)(2,1)S(1)} %constant_dynamic-update-slice_fusion.1), channel_id=1, source_target_pairs={{0,4},{1,5},{2,6},{3,7},{8,12},{9,13},{10,14},{11,15},{16,20},{17,... | collective-permute-start | bytes 2654216 | tf_op jit(solution)/shard_map/ppermute | solution.py:23
  37.1 46.6 %collective-permute-start.7 = (bf16[3,1,384,384]{3,2,1,0:T(8,128)(2,1)S(1)}, bf16[3,1,384,384]{3,2,1,0:T(8,128)(2,1)}, u32[]{:S(2)}, u32[]{:S(2)}) collective-permute-start(bf16[3,1,384,384]{3,2,1,0:T(8,128)(2,1)S(1)} %constant_dynamic-update-slice_fusion.1), channel_id=1, source_target_pairs={{4,0},{5,1},{6,2},{7,3},{12,8},{13,9},{14,10},{15,11},{20,16},{21,... | collective-permute-start | bytes 2654216 | tf_op jit(solution)/shard_map/ppermute | solution.py:25
  39.0 5.2 collective-permute-start
  44.3 5.4 collective-permute-start.1
  51.0 12.1 %collective-permute-start.2 = (bf16[3,1,1]{0,2,1:T(2,128)(2,1)S(1)}, bf16[3,1,1]{0,2,1:T(2,128)(2,1)S(1)}, u32[]{:S(2)}, u32[]{:S(2)}) collective-permute-start(bf16[3,1,1]{0,2,1:T(2,128)(2,1)S(1)} %pad_maximum_fusion.2), channel_id=1, source_target_pairs={{0,4},{1,5},{2,6},{3,7},{8,12},{9,13},{10,14},{11,15},{16,20},{17,... | collective-permute-start | bytes 26 | tf_op jit(solution)/shard_map/ppermute | solution.py:23
  63.1 5.4 collective-permute-start.3
  94.7 3.9 copy-start.7
  117.9 34.0 %copy-start.9 = (f32[1536]{0:T(1024)S(1)}, f32[1536]{0:T(1024)}, u32[]{:S(2)}) copy-start(f32[1536]{0:T(1024)} %param.19) | copy-start | bytes 18436
  117.9 52.5 %all-gather.7.cloned.1.call-start = ((), (), s32[]{:S(2)}) async-start(), calls=%async_computation.5 | async-start | bytes 1474560 | tf_op jit(solution)/shard_map/all_gather | solution.py:144
  152.8 100.0 %all-gather.9.cloned.1.call-start = ((), (), s32[]{:S(2)}) async-start(), calls=%async_computation.6 | async-start | bytes 5308416 | tf_op jit(solution)/shard_map/all_gather | solution.py:146
  153.6 179.6 %all-gather.5.cloned.1.call-start = ((), (), s32[]{:S(2)}) async-start(), calls=%async_computation.3 | async-start | bytes 5308416 | tf_op jit(solution)/shard_map/all_gather | solution.py:147
  154.2 220.4 %reduce-scatter.6.cloned.1.call-start = ((), (), s32[]{:S(2)}) async-start(), calls=%async_computation.7 | async-start | bytes 2949120 | tf_op jit(solution)/shard_map/reduce_scatter | solution.py:153
  343.2 52.6 %all-gather.11.cloned.1.call-start = ((), (), s32[]{:S(2)}) async-start(), calls=%async_computation.8 | async-start | bytes 1474560 | tf_op jit(solution)/shard_map/all_gather | solution.py:158
  378.1 162.6 %reduce-scatter.8.cloned.1.call-start = ((), (), s32[]{:S(2)}) async-start(), calls=%async_computation.9 | async-start | bytes 2654208 | tf_op jit(solution)/shard_map/reduce_scatter | solution.py:162
  395.8 2.4 copy-start.3
  408.4 1.9 copy-start.5
  411.3 1.5 copy-start.6
  423.0 1.9 copy-start.5
  425.9 1.5 copy-start.6
  437.6 1.9 copy-start.5
  440.5 1.5 copy-start.6
  454.6 59.0 %collective-permute-start.16 = (bf16[3,384,384]{2,1,0:T(8,128)(2,1)}, bf16[3,384,384]{2,1,0:T(8,128)(2,1)}, u32[]{:S(2)}, u32[]{:S(2)}) collective-permute-start(bf16[3,384,384]{2,1,0:T(8,128)(2,1)} %squeeze.58), channel_id=1, source_target_pairs={{8,0},{16,8},{24,16},{9,1},{17,9},{25,17},{10,2},{18,10},{26,18},{... | collective-permute-start | bytes 2654216 | tf_op jit(solution)/shard_map/ppermute | solution.py:35
  463.6 50.0 %collective-permute-start.17 = (bf16[3,384,384]{2,1,0:T(8,128)(2,1)}, bf16[3,384,384]{2,1,0:T(8,128)(2,1)}, u32[]{:S(2)}, u32[]{:S(2)}) collective-permute-start(bf16[3,384,384]{2,1,0:T(8,128)(2,1)} %squeeze.59), channel_id=1, source_target_pairs={{0,8},{8,16},{16,24},{1,9},{9,17},{17,25},{2,10},{10,18},{18,26},{... | collective-permute-start | bytes 2654216 | tf_op jit(solution)/shard_map/ppermute | solution.py:35
  480.0 44.5 %collective-permute-start.12 = (bf16[3,384,384]{2,1,0:T(8,128)(2,1)}, bf16[3,384,384]{2,1,0:T(8,128)(2,1)}, u32[]{:S(2)}, u32[]{:S(2)}) collective-permute-start(bf16[3,384,384]{2,1,0:T(8,128)(2,1)} %squeeze.55), channel_id=1, source_target_pairs={{8,0},{16,8},{24,16},{9,1},{17,9},{25,17},{10,2},{18,10},{26,18},{... | collective-permute-start | bytes 2654216 | tf_op jit(solution)/shard_map/ppermute | solution.py:35
  488.9 35.6 %collective-permute-start.13 = (bf16[3,384,384]{2,1,0:T(8,128)(2,1)}, bf16[3,384,384]{2,1,0:T(8,128)(2,1)}, u32[]{:S(2)}, u32[]{:S(2)}) collective-permute-start(bf16[3,384,384]{2,1,0:T(8,128)(2,1)} %squeeze.56), channel_id=1, source_target_pairs={{0,8},{8,16},{16,24},{1,9},{9,17},{17,25},{2,10},{10,18},{18,26},{... | collective-permute-start | bytes 2654216 | tf_op jit(solution)/shard_map/ppermute | solution.py:35
  500.5 4.3 copy-start.2
  517.9 17.8 %collective-permute-start.18 = (bf16[384,384]{1,0:T(8,128)(2,1)}, bf16[384,384]{1,0:T(8,128)(2,1)S(1)}, u32[]{:S(2)}, u32[]{:S(2)}) collective-permute-start(bf16[384,384]{1,0:T(8,128)(2,1)} %get-tuple-element.262), channel_id=1, source_target_pairs={{4,0},{5,1},{6,2},{7,3},{12,8},{13,9},{14,10},{15,11},{20,16},{21,... | collective-permute-start | bytes 884744 | tf_op jit(solution)/shard_map/ppermute | solution.py:35
  519.2 16.5 %collective-permute-start.19 = (bf16[384,384]{1,0:T(8,128)(2,1)S(1)}, bf16[384,384]{1,0:T(8,128)(2,1)}, u32[]{:S(2)}, u32[]{:S(2)}) collective-permute-start(bf16[384,384]{1,0:T(8,128)(2,1)S(1)} %get-tuple-element.263), channel_id=1, source_target_pairs={{0,4},{1,5},{2,6},{3,7},{8,12},{9,13},{10,14},{11,15},{16,20},{17,... | collective-permute-start | bytes 884744 | tf_op jit(solution)/shard_map/ppermute | solution.py:35
  527.5 13.3 %copy-start.4 = (bf16[384,1536]{1,0:T(8,128)(2,1)S(1)}, bf16[384,1536]{1,0:T(8,128)(2,1)}, u32[]{:S(2)}) copy-start(bf16[384,1536]{1,0:T(8,128)(2,1)} %all-gather.11.cloned.1.call-done) | copy-start | bytes 3538948
  528.2 9.5 %collective-permute-start.14 = (bf16[384,384]{1,0:T(8,128)(2,1)}, bf16[384,384]{1,0:T(8,128)(2,1)S(1)}, u32[]{:S(2)}, u32[]{:S(2)}) collective-permute-start(bf16[384,384]{1,0:T(8,128)(2,1)} %get-tuple-element.264), channel_id=1, source_target_pairs={{4,0},{5,1},{6,2},{7,3},{12,8},{13,9},{14,10},{15,11},{20,16},{21,... | collective-permute-start | bytes 884744 | tf_op jit(solution)/shard_map/ppermute | solution.py:35
  529.5 9.2 %collective-permute-start.15 = (bf16[384,384]{1,0:T(8,128)(2,1)S(1)}, bf16[384,384]{1,0:T(8,128)(2,1)}, u32[]{:S(2)}, u32[]{:S(2)}) collective-permute-start(bf16[384,384]{1,0:T(8,128)(2,1)S(1)} %get-tuple-element.265), channel_id=1, source_target_pairs={{0,4},{1,5},{2,6},{3,7},{8,12},{9,13},{10,14},{11,15},{16,20},{17,... | collective-permute-start | bytes 884744 | tf_op jit(solution)/shard_map/ppermute | solution.py:35
  535.7 6.0 %copy-start.1 = (bf16[384,1536]{1,0:T(8,128)(2,1)S(1)}, bf16[384,1536]{1,0:T(8,128)(2,1)}, u32[]{:S(2)}) copy-start(bf16[384,1536]{1,0:T(8,128)(2,1)} %param.18) | copy-start | bytes 3538948
Sparse Core Ops, SparseCore 0:
  118.1 32.2 reduce-scatter.3
  153.0 17.4 all-gather.6
  172.9 79.8 all-gather.8
  255.1 78.0 all-gather.4
  343.3 31.1 reduce-scatter.5
  378.3 17.4 all-gather.10
  400.6 72.8 reduce-scatter.7
where the time goes:
time: 557 us; the launch traced here: 549 us
  waiting for transfers between devices  274 us (49%)
  local copies, waits for them, and re-layouts  84.7 us (15%)
  matrix products  66.8 us (12%)
  starting transfers between devices  66.1 us (12%)
  other arithmetic  41.6 us (7%)
  between operations  15.4 us (3%)
    all_gather x1, waiting for transfers between devices, shards(): lax.all_gather(up_weight, ('ta', 'ha'), axis=0, tiled=True)  82.3 us
    all_gather x1, waiting for transfers between devices, shards(): lax.all_gather(down_weight, ('ta', 'ha'), axis=1, tiled=True)  74.3 us
    reduce_scatter x1, waiting for transfers between devices, shards(): lax.psum_scatter(attn_part, 'wa', scatter_dimension=0, tiled=True)  32.4 us
    reduce_scatter x1, waiting for transfers between devices, shards(): lax.psum_scatter(norm_part, 'wa', scatter_dimension=0, tiled=True)  31.3 us
    ppermute x6, starting transfers between devices, extended(): lax.ppermute(tail, axis, [(i, (i + 1) % count) for i in range(ends)])  30.7 us
    ppermute x8, starting transfers between devices, from_behind(): return lax.ppermute(array, axis, pairs)  27 us
    all_gather x1, waiting for transfers between devices, shards(): stream_grad = lax.all_gather(grad_share, 'wa', axis=0, tiled=True)  17.5 us
    all_gather x1, waiting for transfers between devices, shards(): hidden_in = lax.all_gather(hidden_share, 'wa', axis=0, tiled=True)  15.8 us
  transfers between devices with their start and end apart: 27, of which 12 were waited for; matrix products, arithmetic and copies ran while one was open for 24% of the time, Pallas kernels for 0%

commit v1 on v0

--- a/solution.py
+++ b/solution.py
@@ -10,6 +10,12 @@
 TANH_SCALE = 0.7978845608028654
 CUBIC_COEF = 0.044715
 NEG_FILL = -1e30
+
+
+def laid_out(tiles, dim):
+    tiles = jnp.moveaxis(tiles, 0, dim)
+    shape = tiles.shape
+    return tiles.reshape(*shape[:dim], shape[dim] * shape[dim + 1], *shape[dim + 2 :])
 
 
 def extended(cells, sides, width):
@@ -141,7 +147,19 @@
     )
     normed, inv_std = layer_norm(residual)
     hidden_share = (normed * norm_gain).astype(jnp.bfloat16)
-    hidden_in = lax.all_gather(hidden_share, "wa", axis=0, tiled=True)
+    size = lax.axis_size("wa")
+    pairs_2 = [(i_2, (i_2 + 1) % size) for i_2 in range(size)]
+    back = [(b, a) for a, b in pairs_2]
+    lower, upper = ([], [])
+    for step in range(size - 1):
+        if step % 2 == 0:
+            lower.append(lax.ppermute(lower[-1] if lower else hidden_share, "wa", pairs_2))
+        else:
+            upper.append(lax.ppermute(upper[-1] if upper else hidden_share, "wa", back))
+    parts = jnp.stack([*lower[::-1], hidden_share, *upper])
+    shift = lax.axis_index("wa") - len(lower)
+    parts = parts[(jnp.arange(size) - shift) % size]
+    hidden_in = laid_out(parts, 0)
     up_full, down_full = (
         lax.all_gather(up_weight, ("ta", "ha"), axis=0, tiled=True),
         lax.all_gather(down_weight, ("ta", "ha"), axis=1, tiled=True),

time: 557 us -> 508 us (0.912)
  waiting for transfers between devices: 274 us -> 216 us
    all_gather x1, waiting for transfers between devices: 82.3 us -> 29.9 us  [shards(): lax.all_gather(up_weight, ('ta', 'ha'), axis=0, tiled=True)]
    all_gather x1 -> x0, waiting for transfers between devices: 15.8 us -> none  [shards(): hidden_in = lax.all_gather(hidden_share, 'wa', axis=0, tiled=True)]
    ppermute x0 -> x3, waiting for transfers between devices: none -> 11.7 us  [the longest x2 11.7 us: shards(): lax.ppermute(lower[-1] if lower else hidden_share, 'wa', pairs_2)]
    unnamed x26 -> x38, local copies, waits for them, and re-layouts: 12.3 us -> 13.5 us
  transfers between devices with their start and end apart: 27 -> 29, of which waited for: 12 -> 14; matrix products, arithmetic and copies ran while one was open for 24% -> 28% of each run, Pallas kernels for 0% -> 0%
where the time goes in v1:
time: 508 us; the launch traced here: 499 us
  waiting for transfers between devices  216 us (43%)
  local copies, waits for them, and re-layouts  88.5 us (17%)
  starting transfers between devices  68 us (13%)
  matrix products  67.1 us (13%)
  other arithmetic  42.7 us (8%)
  between operations  16.8 us (3%)
    all_gather x1, waiting for transfers between devices, shards(): lax.all_gather(down_weight, ('ta', 'ha'), axis=1, tiled=True)  73.9 us
    reduce_scatter x1, waiting for transfers between devices, shards(): lax.psum_scatter(norm_part, 'wa', scatter_dimension=0, tiled=True)  31.4 us
    reduce_scatter x1, waiting for transfers between devices, shards(): lax.psum_scatter(attn_part, 'wa', scatter_dimension=0, tiled=True)  31.3 us
    ppermute x6, starting transfers between devices, extended(): lax.ppermute(tail, axis, [(i, (i + 1) % count) for i in range(ends)])  30.7 us
    all_gather x1, waiting for transfers between devices, shards(): lax.all_gather(up_weight, ('ta', 'ha'), axis=0, tiled=True)  29.9 us
    ppermute x8, starting transfers between devices, from_behind(): return lax.ppermute(array, axis, pairs)  27.2 us
    all_gather x1, waiting for transfers between devices, shards(): stream_grad = lax.all_gather(grad_share, 'wa', axis=0, tiled=True)  17.6 us
    unnamed x38, local copies, waits for them, and re-layouts  13.5 us
  transfers between devices with their start and end apart: 29, of which 14 were waited for; matrix products, arithmetic and copies ran while one was open for 28% of the time, Pallas kernels for 0%

profile of v1, /device:TPU:0, one launch (start us, length us, event | category | flops | bytes accessed | tf_op | source)
XLA Modules:
  0.0 499.4 jit_solution(17781928242858018217)
XLA Ops:
  8.1 5.1 %collective-permute-start.8 = (bf16[1,1,384,384]{3,2,1,0:T(8,128)(2,1)}, bf16[1,1,384,384]{3,2,1,0:T(8,128)(2,1)S(1)}, u32[]{:S(2)}, u32[]{:S(2)}) collective-permute-start(bf16[1,1,384,384]{3,2,1,0:T(8,128)(2,1)} %param.17), channel_id=1, source_target_pairs={{0,8},{8,16},{16,24},{1,9},{9,17},{17,25},{2,10},{10,18},{18,26},{... | collective-permute-start | bytes 884744 | tf_op jit(solution)/shard_map/ppermute | solution.py:29
  14.5 4.6 collective-permute-start.4
  21.7 3.0 collective-permute-done.9
  24.7 4.4 collective-permute-start.10
  31.5 6.4 %collective-permute-start.6 = (bf16[3,1,384,384]{3,2,1,0:T(8,128)(2,1)S(1)}, bf16[3,1,384,384]{3,2,1,0:T(8,128)(2,1)}, u32[]{:S(2)}, u32[]{:S(2)}) collective-permute-start(bf16[3,1,384,384]{3,2,1,0:T(8,128)(2,1)S(1)} %constant_dynamic-update-slice_fusion.1), channel_id=1, source_target_pairs={{0,4},{1,5},{2,6},{3,7},{8,12},{9,13},{10,14},{11,15},{16,20},{17,... | collective-permute-start | bytes 2654216 | tf_op jit(solution)/shard_map/ppermute | solution.py:29
  39.9 4.8 collective-permute-start
  46.4 4.2 collective-permute-done.1
  51.9 5.5 %collective-permute-start.2 = (bf16[3,1,1]{0,2,1:T(2,128)(2,1)S(1)}, bf16[3,1,1]{0,2,1:T(2,128)(2,1)S(1)}, u32[]{:S(2)}, u32[]{:S(2)}) collective-permute-start(bf16[3,1,1]{0,2,1:T(2,128)(2,1)S(1)} %pad_maximum_fusion.3), channel_id=1, source_target_pairs={{0,4},{1,5},{2,6},{3,7},{8,12},{9,13},{10,14},{11,15},{16,20},{17,... | collective-permute-start | bytes 26 | tf_op jit(solution)/shard_map/ppermute | solution.py:29
  57.4 6.5 %collective-permute-done.2 = bf16[3,1,1]{0,2,1:T(2,128)(2,1)S(1)} collective-permute-done((bf16[3,1,1]{0,2,1:T(2,128)(2,1)S(1)}, bf16[3,1,1]{0,2,1:T(2,128)(2,1)S(1)}, u32[]{:S(2)}, u32[]{:S(2)}) %collective-permute-start.2) | collective-permute-done | bytes 38 | tf_op jit(solution)/shard_map/ppermute | solution.py:29
  65.3 4.0 collective-permute-done.3
  69.6 3.3 pad_maximum_fusion.1
  72.9 7.7 %reshape.199 = bf16[3456,3,128]{2,1,0:T(4,128)(2,1)} reshape(bf16[3,3,384,384]{3,2,1,0:T(8,128)(2,1)} %pad_maximum_fusion.1) | data formatting | bytes 5308416 | tf_op jit(solution)/shard_map/while/body/eval_jaxpr/reshape | solution.py:109
  80.7 3.9 copy.47
  84.6 3.3 pad_maximum_fusion
  87.9 7.7 %reshape.198 = bf16[3456,3,128]{2,1,0:T(4,128)(2,1)} reshape(bf16[3,3,384,384]{3,2,1,0:T(8,128)(2,1)} %pad_maximum_fusion) | data formatting | bytes 5308416 | tf_op jit(solution)/shard_map/while/body/eval_jaxpr/reshape | solution.py:108
  95.6 3.9 copy.46
  99.6 16.9 %while.44 = (s32[]{:T(128)}, f32[3,384,128]{1,2,0:T(8,128)S(1)}, bf16[3,384,128]{2,1,0:T(8,128)(2,1)S(1)}, bf16[3,3456,128]{2,1,0:T(8,128)(2,1)}, bf16[3,3456,128]{2,1,0:T(8,128)(2,1)}, /*index=5*/f32[9]{0:T(128)S(1)}, s32[]{:T(128)}) while((s32[]{:T(128)}, f32[3,384,128]{1,2,0:T(8,128)S(1)}, bf16[3,384,128]{2,1,0:T(8,128)(2,1)S(1)}, ...), condition=%wide.region_3.4_spmd.clone, body=%wide.region_0.3_spmd.clone.sunk | while | flops 690093312 | bytes 18014980 | solution.py:132
  99.7 2.2 fusion.113
  102.7 2.5 fusion.115
  105.3 2.2 fusion.113
  108.4 2.5 fusion.115
  111.0 2.2 fusion.113
  114.0 2.5 fusion.115
  117.1 2.2 fusion.81
  120.5 31.3 %reduce-scatter.4.cloned.1.call-done = f32[96,1536]{1,0:T(8,128)} async-done(((f32[384,1536]{1,0:T(8,128)}), f32[96,1536]{1,0:T(8,128)}) %reduce-scatter.4.cloned.1.call-update) | async-done | bytes 589840 | tf_op jit(solution)/shard_map/reduce_scatter | solution.py:139
  156.0 5.7 %collective-permute-done.12 = bf16[96,1536]{1,0:T(8,128)(2,1)S(1)} collective-permute-done((bf16[96,1536]{1,0:T(8,128)(2,1)S(1)}, bf16[96,1536]{1,0:T(8,128)(2,1)S(1)}, u32[]{:S(2)}, u32[]{:S(2)}) %collective-permute-start.12) | collective-permute-done | bytes 294944 | tf_op jit(solution)/shard_map/ppermute | solution.py:156
  162.3 6.0 %collective-permute-done.13 = bf16[96,1536]{1,0:T(8,128)(2,1)S(1)} collective-permute-done((bf16[96,1536]{1,0:T(8,128)(2,1)S(1)}, bf16[96,1536]{1,0:T(8,128)(2,1)S(1)}, u32[]{:S(2)}, u32[]{:S(2)}) %collective-permute-start.13) | collective-permute-done | bytes 294944 | tf_op jit(solution)/shard_map/ppermute | solution.py:156
  171.1 29.9 %all-gather.6.cloned.1.call-done = bf16[1536,1536]{1,0:T(8,128)(2,1)} async-done(((bf16[192,1536]{1,0:T(8,128)(2,1)}), bf16[1536,1536]{1,0:T(8,128)(2,1)}) %all-gather.6.cloned.1.call-update) | async-done | bytes 4718608 | tf_op jit(solution)/shard_map/all_gather | solution.py:164
  201.0 6.2 %fusion.82 = f32[384,1536]{1,0:T(8,128)} fusion(bf16[384,1536]{1,0:T(8,128)(2,1)} %bitcast.182, bf16[1536,1536]{1,0:T(8,128)(2,1)} %all-gather.6.cloned.1.call-done), kind=kOutput, calls=%fused_computation.133 | convolution fusion | flops 1811939328 | bytes 8257536 | tf_op jit(solution)/shard_map/dot_general | solution.py:167
  207.2 73.9 %all-gather.4.cloned.1.call-done = bf16[1536,1536]{0,1:T(8,128)(2,1)} async-done(((bf16[1536,192]{0,1:T(8,128)(2,1)}), bf16[1536,1536]{0,1:T(8,128)(2,1)}) %all-gather.4.cloned.1.call-update) | async-done | bytes 4718608 | tf_op jit(solution)/shard_map/all_gather | solution.py:165
  281.0 9.6 %fusion.56 = f32[384,1536]{1,0:T(8,128)} fusion(bf16[1536,1536]{1,0:T(8,128)(2,1)} %all-gather.6.cloned.1.call-done, bf16[1536,1536]{0,1:T(8,128)(2,1)} %all-gather.4.cloned.1.call-done, f32[384,1536]{1,0:T(8,128)} %fusion.82, bf16[1,1,384,1536]{3,2,1,0:T(8,128)(2,1)S(1)} %copy-done.13), kind=kOutput, calls=%fused_computation.77 | convolution fusion | flops 3635085312 | bytes 15335424 | tf_op jit(solution)/shard_map/tf,df->td/dot_general | solution.py:170
  290.7 31.4 %reduce-scatter.6.cloned.1.call-done = f32[96,1536]{1,0:T(8,128)} async-done(((f32[384,1536]{1,0:T(8,128)}), f32[96,1536]{1,0:T(8,128)}) %reduce-scatter.6.cloned.1.call-update) | async-done | bytes 589840 | tf_op jit(solution)/shard_map/reduce_scatter | solution.py:171
  323.5 2.1 fusion.64
  325.7 17.6 %all-gather.8.cloned.1.call-done = bf16[384,1536]{1,0:T(8,128)(2,1)} async-done(((bf16[96,1536]{1,0:T(8,128)(2,1)}), bf16[384,1536]{1,0:T(8,128)(2,1)}) %all-gather.8.cloned.1.call-update) | async-done | bytes 1179664 | tf_op jit(solution)/shard_map/all_gather | solution.py:176
  343.3 2.9 fusion.54
  347.3 2.4 fusion.83
  349.7 43.6 %while.45 = (s32[]{:T(128)}, bf16[3,384,128]{1,2,0:T(8,128)(2,1)S(1)}, bf16[3,3456,128]{2,1,0:T(8,128)(2,1)}, bf16[3,3456,128]{2,1,0:T(8,128)(2,1)}, bf16[3,384,...) while((s32[]{:T(128)}, ...), condition=%wide.region_14.15_spmd.clone, body=%wide.region_10.14_spmd.clone.sunk | while | flops 1723513728 | bytes 71701848 | solution.py:215
  349.9 2.2 fusion.122
  352.9 2.2 fusion.126
  355.1 2.5 multiply_reduce_fusion.5
  364.4 2.2 fusion.122
  367.5 2.2 fusion.126
  369.6 2.5 multiply_reduce_fusion.5
  378.9 2.2 fusion.122
  382.0 2.2 fusion.126
  384.2 2.5 multiply_reduce_fusion.5
  391.2 2.0 fusion.124
  394.1 2.8 fusion.79
  396.9 5.5 %copy.58 = bf16[1152,3,128]{2,1,0:T(4,128)(2,1)S(1)} copy(bf16[1152,3,128]{2,0,1:T(8,128)(2,1)S(1)} %get-tuple-element.256) | data formatting | bytes 1769472 | tf_op jit(solution)/shard_map/slice | solution.py:244
  405.8 5.6 %copy.59 = bf16[1152,3,128]{2,1,0:T(4,128)(2,1)S(1)} copy(bf16[1152,3,128]{2,0,1:T(8,128)(2,1)} %get-tuple-element.257) | data formatting | bytes 1769472 | tf_op jit(solution)/shard_map/slice | solution.py:244
  413.4 5.5 %collective-permute-start.20 = (bf16[3,384,384]{2,1,0:T(8,128)(2,1)}, bf16[3,384,384]{2,1,0:T(8,128)(2,1)}, u32[]{:S(2)}, u32[]{:S(2)}) collective-permute-start(bf16[3,384,384]{2,1,0:T(8,128)(2,1)} %squeeze.59), channel_id=1, source_target_pairs={{0,8},{8,16},{16,24},{1,9},{9,17},{17,25},{2,10},{10,18},{18,26},{... | collective-permute-start | bytes 2654216 | tf_op jit(solution)/shard_map/ppermute | solution.py:41
  418.9 3.5 fusion.80
  422.4 5.5 %copy.55 = bf16[1152,3,128]{2,1,0:T(4,128)(2,1)S(1)} copy(bf16[1152,3,128]{2,0,1:T(8,128)(2,1)S(1)} %get-tuple-element.259) | data formatting | bytes 1769472 | tf_op jit(solution)/shard_map/slice | solution.py:244
  431.1 5.6 %copy.56 = bf16[1152,3,128]{2,1,0:T(4,128)(2,1)S(1)} copy(bf16[1152,3,128]{2,0,1:T(8,128)(2,1)} %get-tuple-element.260) | data formatting | bytes 1769472 | tf_op jit(solution)/shard_map/slice | solution.py:244
  438.7 5.7 %collective-permute-start.16 = (bf16[3,384,384]{2,1,0:T(8,128)(2,1)}, bf16[3,384,384]{2,1,0:T(8,128)(2,1)}, u32[]{:S(2)}, u32[]{:S(2)}) collective-permute-start(bf16[3,384,384]{2,1,0:T(8,128)(2,1)} %squeeze.56), channel_id=1, source_target_pairs={{0,8},{8,16},{16,24},{1,9},{9,17},{17,25},{2,10},{10,18},{18,26},{... | collective-permute-start | bytes 2654216 | tf_op jit(solution)/shard_map/ppermute | solution.py:41
  444.3 5.9 %copy.57 = f32[1152,3,128]{2,1,0:T(4,128)} copy(f32[1152,3,128]{2,0,1:T(8,128)S(1)} %get-tuple-element.258) | data formatting | bytes 3538944 | tf_op jit(solution)/shard_map/convert_element_type | solution.py:241
  450.3 4.3 reshape.211
  454.5 5.9 %copy.54 = f32[1152,3,128]{2,1,0:T(4,128)} copy(f32[1152,3,128]{2,0,1:T(8,128)S(1)} %copy-done.2) | data formatting | bytes 3538944 | tf_op jit(solution)/shard_map/convert_element_type | solution.py:240
  460.4 3.0 reshape.210
  463.4 3.6 fusion.74
  469.0 5.4 %collective-permute-start.22 = (bf16[384,384]{1,0:T(8,128)(2,1)S(1)}, bf16[384,384]{1,0:T(8,128)(2,1)}, u32[]{:S(2)}, u32[]{:S(2)}) collective-permute-start(bf16[384,384]{1,0:T(8,128)(2,1)S(1)} %get-tuple-element.263), channel_id=1, source_target_pairs={{0,4},{1,5},{2,6},{3,7},{8,12},{9,13},{10,14},{11,15},{16,20},{17,... | collective-permute-start | bytes 884744 | tf_op jit(solution)/shard_map/ppermute | solution.py:41
  474.5 2.9 fusion.75
  479.5 5.3 %collective-permute-start.18 = (bf16[384,384]{1,0:T(8,128)(2,1)S(1)}, bf16[384,384]{1,0:T(8,128)(2,1)}, u32[]{:S(2)}, u32[]{:S(2)}) collective-permute-start(bf16[384,384]{1,0:T(8,128)(2,1)S(1)} %get-tuple-element.265), channel_id=1, source_target_pairs={{0,4},{1,5},{2,6},{3,7},{8,12},{9,13},{10,14},{11,15},{16,20},{17,... | collective-permute-start | bytes 884744 | tf_op jit(solution)/shard_map/ppermute | solution.py:41
  485.7 2.1 fusion.66
  (162 shorter events, 68.3 us)
Async XLA Ops:
  8.0 109.1 %copy-start = (bf16[384,1536]{1,0:T(8,128)(2,1)S(1)}, bf16[384,1536]{1,0:T(8,128)(2,1)}, u32[]{:S(2)}) copy-start(bf16[384,1536]{1,0:T(8,128)(2,1)} %param.18) | copy-start | bytes 3538948
  8.0 36.6 %copy-start.9 = (bf16[1,1,384,384]{3,2,1,0:T(8,128)(2,1)S(1)}, bf16[1,1,384,384]{3,2,1,0:T(8,128)(2,1)}, u32[]{:S(2)}) copy-start(bf16[1,1,384,384]{3,2,1,0:T(8,128)(2,1)} %param.15) | copy-start | bytes 884740
  8.0 143.8 %reduce-scatter.4.cloned.1.call-start = ((), (), s32[]{:S(2)}) async-start(), calls=%async_computation.4 | async-start | bytes 2949120 | tf_op jit(solution)/shard_map/reduce_scatter | solution.py:139
  8.1 12.6 %collective-permute-start.8 = (bf16[1,1,384,384]{3,2,1,0:T(8,128)(2,1)}, bf16[1,1,384,384]{3,2,1,0:T(8,128)(2,1)S(1)}, u32[]{:S(2)}, u32[]{:S(2)}) collective-permute-start(bf16[1,1,384,384]{3,2,1,0:T(8,128)(2,1)} %param.17), channel_id=1, source_target_pairs={{0,8},{8,16},{16,24},{1,9},{9,17},{17,25},{2,10},{10,18},{18,26},{... | collective-permute-start | bytes 884744 | tf_op jit(solution)/shard_map/ppermute | solution.py:29
  13.2 11.5 %collective-permute-start.9 = (bf16[1,1,384,384]{3,2,1,0:T(8,128)(2,1)}, bf16[1,1,384,384]{3,2,1,0:T(8,128)(2,1)S(1)}, u32[]{:S(2)}, u32[]{:S(2)}) collective-permute-start(bf16[1,1,384,384]{3,2,1,0:T(8,128)(2,1)} %param.17), channel_id=1, source_target_pairs={{8,0},{16,8},{24,16},{9,1},{17,9},{25,17},{10,2},{18,10},{26,18},{... | collective-permute-start | bytes 884744 | tf_op jit(solution)/shard_map/ppermute | solution.py:31
  14.5 15.9 %collective-permute-start.4 = (bf16[1,1,384,384]{3,2,1,0:T(8,128)(2,1)}, bf16[1,1,384,384]{3,2,1,0:T(8,128)(2,1)S(1)}, u32[]{:S(2)}, u32[]{:S(2)}) collective-permute-start(bf16[1,1,384,384]{3,2,1,0:T(8,128)(2,1)} %param.16), channel_id=1, source_target_pairs={{0,8},{8,16},{16,24},{1,9},{9,17},{17,25},{2,10},{10,18},{18,26},{... | collective-permute-start | bytes 884744 | tf_op jit(solution)/shard_map/ppermute | solution.py:29
  19.0 12.4 %collective-permute-start.5 = (bf16[1,1,384,384]{3,2,1,0:T(8,128)(2,1)}, bf16[1,1,384,384]{3,2,1,0:T(8,128)(2,1)S(1)}, u32[]{:S(2)}, u32[]{:S(2)}) collective-permute-start(bf16[1,1,384,384]{3,2,1,0:T(8,128)(2,1)} %param.16), channel_id=1, source_target_pairs={{8,0},{16,8},{24,16},{9,1},{17,9},{25,17},{10,2},{18,10},{26,18},{... | collective-permute-start | bytes 884744 | tf_op jit(solution)/shard_map/ppermute | solution.py:31
  24.7 44.9 %collective-permute-start.10 = (bf16[3,1,384,384]{3,2,1,0:T(8,128)(2,1)S(1)}, bf16[3,1,384,384]{3,2,1,0:T(8,128)(2,1)}, u32[]{:S(2)}, u32[]{:S(2)}) collective-permute-start(bf16[3,1,384,384]{3,2,1,0:T(8,128)(2,1)S(1)} %constant_dynamic-update-slice_fusion.4), channel_id=1, source_target_pairs={{0,4},{1,5},{2,6},{3,7},{8,12},{9,13},{10,14},{11,15},{16,20},{17,... | collective-permute-start | bytes 2654216 | tf_op jit(solution)/shard_map/ppermute | solution.py:29
  29.1 40.5 %collective-permute-start.11 = (bf16[3,1,384,384]{3,2,1,0:T(8,128)(2,1)S(1)}, bf16[3,1,384,384]{3,2,1,0:T(8,128)(2,1)}, u32[]{:S(2)}, u32[]{:S(2)}) collective-permute-start(bf16[3,1,384,384]{3,2,1,0:T(8,128)(2,1)S(1)} %constant_dynamic-update-slice_fusion.4), channel_id=1, source_target_pairs={{4,0},{5,1},{6,2},{7,3},{12,8},{13,9},{14,10},{15,11},{20,16},{21,... | collective-permute-start | bytes 2654216 | tf_op jit(solution)/shard_map/ppermute | solution.py:31
  31.5 53.1 %collective-permute-start.6 = (bf16[3,1,384,384]{3,2,1,0:T(8,128)(2,1)S(1)}, bf16[3,1,384,384]{3,2,1,0:T(8,128)(2,1)}, u32[]{:S(2)}, u32[]{:S(2)}) collective-permute-start(bf16[3,1,384,384]{3,2,1,0:T(8,128)(2,1)S(1)} %constant_dynamic-update-slice_fusion.1), channel_id=1, source_target_pairs={{0,4},{1,5},{2,6},{3,7},{8,12},{9,13},{10,14},{11,15},{16,20},{17,... | collective-permute-start | bytes 2654216 | tf_op jit(solution)/shard_map/ppermute | solution.py:29
  37.9 46.6 %collective-permute-start.7 = (bf16[3,1,384,384]{3,2,1,0:T(8,128)(2,1)S(1)}, bf16[3,1,384,384]{3,2,1,0:T(8,128)(2,1)}, u32[]{:S(2)}, u32[]{:S(2)}) collective-permute-start(bf16[3,1,384,384]{3,2,1,0:T(8,128)(2,1)S(1)} %constant_dynamic-update-slice_fusion.1), channel_id=1, source_target_pairs={{4,0},{5,1},{6,2},{7,3},{12,8},{13,9},{14,10},{15,11},{20,16},{21,... | collective-permute-start | bytes 2654216 | tf_op jit(solution)/shard_map/ppermute | solution.py:31
  39.9 5.2 %collective-permute-start = (bf16[1,1,1]{0,2,1:T(2,128)(2,1)}, bf16[1,1,1]{0,2,1:T(2,128)(2,1)}, u32[]{:S(2)}, u32[]{:S(2)}) collective-permute-start(bf16[1,1,1]{0,2,1:T(2,128)(2,1)} %convert_element_type.124), channel_id=1, source_target_pairs={{0,8},{8,16},{16,24},{1,9},{9,17},{17,25},{2,10},{10,18},{18,26},{... | collective-permute-start | bytes 14 | tf_op jit(solution)/shard_map/ppermute | solution.py:29
  45.1 5.5 %collective-permute-start.1 = (bf16[1,1,1]{0,2,1:T(2,128)(2,1)}, bf16[1,1,1]{0,2,1:T(2,128)(2,1)}, u32[]{:S(2)}, u32[]{:S(2)}) collective-permute-start(bf16[1,1,1]{0,2,1:T(2,128)(2,1)} %convert_element_type.124), channel_id=1, source_target_pairs={{8,0},{16,8},{24,16},{9,1},{17,9},{25,17},{10,2},{18,10},{26,18},{... | collective-permute-start | bytes 14 | tf_op jit(solution)/shard_map/ppermute | solution.py:31
  51.9 12.1 %collective-permute-start.2 = (bf16[3,1,1]{0,2,1:T(2,128)(2,1)S(1)}, bf16[3,1,1]{0,2,1:T(2,128)(2,1)S(1)}, u32[]{:S(2)}, u32[]{:S(2)}) collective-permute-start(bf16[3,1,1]{0,2,1:T(2,128)(2,1)S(1)} %pad_maximum_fusion.3), channel_id=1, source_target_pairs={{0,4},{1,5},{2,6},{3,7},{8,12},{9,13},{10,14},{11,15},{16,20},{17,... | collective-permute-start | bytes 26 | tf_op jit(solution)/shard_map/ppermute | solution.py:29
  63.9 5.4 %collective-permute-start.3 = (bf16[3,1,1]{0,2,1:T(2,128)(2,1)S(1)}, bf16[3,1,1]{0,2,1:T(2,128)(2,1)S(1)}, u32[]{:S(2)}, u32[]{:S(2)}) collective-permute-start(bf16[3,1,1]{0,2,1:T(2,128)(2,1)S(1)} %pad_maximum_fusion.3), channel_id=1, source_target_pairs={{4,0},{5,1},{6,2},{7,3},{12,8},{13,9},{14,10},{15,11},{20,16},{21,... | collective-permute-start | bytes 26 | tf_op jit(solution)/shard_map/ppermute | solution.py:31
  95.6 3.9 copy-start.7
  116.5 0.5 copy-start.14
  119.3 34.1 %copy-start.12 = (f32[1536]{0:T(1024)S(1)}, f32[1536]{0:T(1024)}, u32[]{:S(2)}) copy-start(f32[1536]{0:T(1024)} %param.19) | copy-start | bytes 18436
  119.3 81.7 %all-gather.6.cloned.1.call-start = ((), (), s32[]{:S(2)}) async-start(), calls=%async_computation.5 | async-start | bytes 5308416 | tf_op jit(solution)/shard_map/all_gather | solution.py:164
  119.9 161.1 %all-gather.4.cloned.1.call-start = ((), (), s32[]{:S(2)}) async-start(), calls=%async_computation.3 | async-start | bytes 5308416 | tf_op jit(solution)/shard_map/all_gather | solution.py:165
  120.5 201.6 %reduce-scatter.6.cloned.1.call-start = ((), (), s32[]{:S(2)}) async-start(), calls=%async_computation.6 | async-start | bytes 2949120 | tf_op jit(solution)/shard_map/reduce_scatter | solution.py:171
  153.5 8.1 %collective-permute-start.12 = (bf16[96,1536]{1,0:T(8,128)(2,1)S(1)}, bf16[96,1536]{1,0:T(8,128)(2,1)S(1)}, u32[]{:S(2)}, u32[]{:S(2)}) collective-permute-start(bf16[96,1536]{1,0:T(8,128)(2,1)S(1)} %multiply_convert_fusion.1), channel_id=1, source_target_pairs={{0,1},{1,2},{2,3},{3,0},{4,5},{5,6},{6,7},{7,4},{8,9},{9,10},{10,1... | collective-permute-start | bytes 884744 | tf_op jit(solution)/shard_map/ppermute | solution.py:156
  154.2 8.0 %collective-permute-start.14 = (bf16[96,1536]{1,0:T(8,128)(2,1)S(1)}, bf16[96,1536]{1,0:T(8,128)(2,1)S(1)}, u32[]{:S(2)}, u32[]{:S(2)}) collective-permute-start(bf16[96,1536]{1,0:T(8,128)(2,1)S(1)} %multiply_convert_fusion.1), channel_id=1, source_target_pairs={{1,0},{2,1},{3,2},{0,3},{5,4},{6,5},{7,6},{4,7},{9,8},{10,9},{11,1... | collective-permute-start | bytes 884744 | tf_op jit(solution)/shard_map/ppermute | solution.py:158
  161.7 6.6 %copy-start.8 = (bf16[96,1536]{1,0:T(8,128)(2,1)}, bf16[96,1536]{1,0:T(8,128)(2,1)S(1)}, u32[]{:S(2)}) copy-start(bf16[96,1536]{1,0:T(8,128)(2,1)S(1)} %collective-permute-done.12) | copy-start | bytes 884740
  161.7 6.6 %collective-permute-start.13 = (bf16[96,1536]{1,0:T(8,128)(2,1)S(1)}, bf16[96,1536]{1,0:T(8,128)(2,1)S(1)}, u32[]{:S(2)}, u32[]{:S(2)}) collective-permute-start(bf16[96,1536]{1,0:T(8,128)(2,1)S(1)} %collective-permute-done.12), channel_id=1, source_target_pairs={{0,1},{1,2},{2,3},{3,0},{4,5},{5,6},{6,7},{7,4},{8,9},{9,10},{10,1... | collective-permute-start | bytes 884744 | tf_op jit(solution)/shard_map/ppermute | solution.py:156
  201.0 80.0 %copy-start.13 = (bf16[1,1,384,1536]{3,2,1,0:T(8,128)(2,1)S(1)}, bf16[1,1,384,1536]{3,2,1,0:T(8,128)(2,1)}, u32[]{:S(2)}) copy-start(bf16[1,1,384,1536]{3,2,1,0:T(8,128)(2,1)} %param.23) | copy-start | bytes 3538948
  290.7 52.6 %all-gather.8.cloned.1.call-start = ((), (), s32[]{:S(2)}) async-start(), calls=%async_computation.7 | async-start | bytes 1474560 | tf_op jit(solution)/shard_map/all_gather | solution.py:176
  325.6 165.2 %reduce-scatter.8.cloned.1.call-start = ((), (), s32[]{:S(2)}) async-start(), calls=%async_computation.8 | async-start | bytes 2654208 | tf_op jit(solution)/shard_map/reduce_scatter | solution.py:180
  343.3 4.0 copy-start.3
  347.3 2.4 copy-start.15
  357.6 1.9 copy-start.5
  360.6 1.5 copy-start.6
  372.1 1.9 copy-start.5
  375.1 1.5 copy-start.6
  386.7 1.9 copy-start.5
  389.7 1.5 copy-start.6
  393.4 0.7 copy-start.10
  404.4 59.0 %collective-permute-start.19 = (bf16[3,384,384]{2,1,0:T(8,128)(2,1)}, bf16[3,384,384]{2,1,0:T(8,128)(2,1)}, u32[]{:S(2)}, u32[]{:S(2)}) collective-permute-start(bf16[3,384,384]{2,1,0:T(8,128)(2,1)} %squeeze.58), channel_id=1, source_target_pairs={{8,0},{16,8},{24,16},{9,1},{17,9},{25,17},{10,2},{18,10},{26,18},{... | collective-permute-start | bytes 2654216 | tf_op jit(solution)/shard_map/ppermute | solution.py:41
  413.4 50.0 %collective-permute-start.20 = (bf16[3,384,384]{2,1,0:T(8,128)(2,1)}, bf16[3,384,384]{2,1,0:T(8,128)(2,1)}, u32[]{:S(2)}, u32[]{:S(2)}) collective-permute-start(bf16[3,384,384]{2,1,0:T(8,128)(2,1)} %squeeze.59), channel_id=1, source_target_pairs={{0,8},{8,16},{16,24},{1,9},{9,17},{17,25},{2,10},{10,18},{18,26},{... | collective-permute-start | bytes 2654216 | tf_op jit(solution)/shard_map/ppermute | solution.py:41
  429.8 44.7 %collective-permute-start.15 = (bf16[3,384,384]{2,1,0:T(8,128)(2,1)}, bf16[3,384,384]{2,1,0:T(8,128)(2,1)}, u32[]{:S(2)}, u32[]{:S(2)}) collective-permute-start(bf16[3,384,384]{2,1,0:T(8,128)(2,1)} %squeeze.55), channel_id=1, source_target_pairs={{8,0},{16,8},{24,16},{9,1},{17,9},{25,17},{10,2},{18,10},{26,18},{... | collective-permute-start | bytes 2654216 | tf_op jit(solution)/shard_map/ppermute | solution.py:41
  438.7 35.8 %collective-permute-start.16 = (bf16[3,384,384]{2,1,0:T(8,128)(2,1)}, bf16[3,384,384]{2,1,0:T(8,128)(2,1)}, u32[]{:S(2)}, u32[]{:S(2)}) collective-permute-start(bf16[3,384,384]{2,1,0:T(8,128)(2,1)} %squeeze.56), channel_id=1, source_target_pairs={{0,8},{8,16},{16,24},{1,9},{9,17},{17,25},{2,10},{10,18},{18,26},{... | collective-permute-start | bytes 2654216 | tf_op jit(solution)/shard_map/ppermute | solution.py:41
  450.3 4.3 copy-start.2
  467.7 17.9 %collective-permute-start.21 = (bf16[384,384]{1,0:T(8,128)(2,1)}, bf16[384,384]{1,0:T(8,128)(2,1)S(1)}, u32[]{:S(2)}, u32[]{:S(2)}) collective-permute-start(bf16[384,384]{1,0:T(8,128)(2,1)} %get-tuple-element.262), channel_id=1, source_target_pairs={{4,0},{5,1},{6,2},{7,3},{12,8},{13,9},{14,10},{15,11},{20,16},{21,... | collective-permute-start | bytes 884744 | tf_op jit(solution)/shard_map/ppermute | solution.py:41
  469.0 15.7 %copy-start.11 = (bf16[3,384,128]{1,2,0:T(8,128)(2,1)S(1)}, bf16[3,384,128]{1,2,0:T(8,128)(2,1)}, u32[]{:S(2)}) copy-start(bf16[3,384,128]{1,2,0:T(8,128)(2,1)} %copy-done.10) | copy-start | bytes 884740
  469.0 16.6 %collective-permute-start.22 = (bf16[384,384]{1,0:T(8,128)(2,1)S(1)}, bf16[384,384]{1,0:T(8,128)(2,1)}, u32[]{:S(2)}, u32[]{:S(2)}) collective-permute-start(bf16[384,384]{1,0:T(8,128)(2,1)S(1)} %get-tuple-element.263), channel_id=1, source_target_pairs={{0,4},{1,5},{2,6},{3,7},{8,12},{9,13},{10,14},{11,15},{16,20},{17,... | collective-permute-start | bytes 884744 | tf_op jit(solution)/shard_map/ppermute | solution.py:41
  477.4 13.4 %copy-start.4 = (bf16[384,1536]{1,0:T(8,128)(2,1)S(1)}, bf16[384,1536]{1,0:T(8,128)(2,1)}, u32[]{:S(2)}) copy-start(bf16[384,1536]{1,0:T(8,128)(2,1)} %all-gather.8.cloned.1.call-done) | copy-start | bytes 3538948
  478.2 9.7 %collective-permute-start.17 = (bf16[384,384]{1,0:T(8,128)(2,1)}, bf16[384,384]{1,0:T(8,128)(2,1)S(1)}, u32[]{:S(2)}, u32[]{:S(2)}) collective-permute-start(bf16[384,384]{1,0:T(8,128)(2,1)} %get-tuple-element.264), channel_id=1, source_target_pairs={{4,0},{5,1},{6,2},{7,3},{12,8},{13,9},{14,10},{15,11},{20,16},{21,... | collective-permute-start | bytes 884744 | tf_op jit(solution)/shard_map/ppermute | solution.py:41
  479.5 9.4 %collective-permute-start.18 = (bf16[384,384]{1,0:T(8,128)(2,1)S(1)}, bf16[384,384]{1,0:T(8,128)(2,1)}, u32[]{:S(2)}, u32[]{:S(2)}) collective-permute-start(bf16[384,384]{1,0:T(8,128)(2,1)S(1)} %get-tuple-element.265), channel_id=1, source_target_pairs={{0,4},{1,5},{2,6},{3,7},{8,12},{9,13},{10,14},{11,15},{16,20},{17,... | collective-permute-start | bytes 884744 | tf_op jit(solution)/shard_map/ppermute | solution.py:41
  485.7 6.2 %copy-start.1 = (bf16[384,1536]{1,0:T(8,128)(2,1)S(1)}, bf16[384,1536]{1,0:T(8,128)(2,1)}, u32[]{:S(2)}) copy-start(bf16[384,1536]{1,0:T(8,128)(2,1)} %param.18) | copy-start | bytes 3538948
Sparse Core Ops, SparseCore 0:
  119.4 32.3 reduce-scatter.3
  290.8 31.2 reduce-scatter.5
  325.8 17.4 all-gather.7
Sparse Core Ops, SparseCore 1:
  122.2 78.7 all-gather.5
  203.3 77.7 all-gather.3
  349.8 72.5 reduce-scatter.7
